TPU v7x, 32 devices: a whole 2x2x4 slice. The times are simulated.
32 devices in a mesh: clip: 8 (over y, x, core), seq: 4 (over z).
Axes of the slice: x: 2, y: 2, z: 4, core: 2. Of those that a mesh axis runs over, the one named last changes fastest.
Arguments:
- tokens: bfloat16 [32, 380, 768], P('clip', 'seq'), may hold values from -6 to 6
- freq_index: int32 [32, 7], P('clip'), may hold values from 0 to 11, as said below
- time_index: int32 [32, 54], P('clip'), may hold values from 0 to 98, as said below
- freq_table: bfloat16 [12, 768], replicated, may hold values from -3 to 3
- time_table: bfloat16 [99, 768], replicated, may hold values from -3 to 3
- norm1_gain: bfloat16 [768], replicated, may hold values from 0.25 to 1.75
- norm1_shift: bfloat16 [768], replicated, may hold values from -2 to 2
- qkv_weight: bfloat16 [768, 2304], replicated, may hold values from -0.21875 to 0.21875
- qv_bias: bfloat16 [2, 768], replicated, may hold values from -2 to 2
- proj_weight: bfloat16 [768, 768], replicated, may hold values from -2.5 to 2.5
- proj_bias: bfloat16 [768], replicated, may hold values from -2 to 2
- norm2_gain: bfloat16 [768], replicated, may hold values from 0.25 to 1.75
- norm2_shift: bfloat16 [768], replicated, may hold values from -2 to 2
- fc1_weight: bfloat16 [768, 3072], replicated, may hold values from -0.21875 to 0.21875
- fc1_bias: bfloat16 [3072], replicated, may hold values from -3 to 3
- fc2_weight: bfloat16 [3072, 768], replicated, may hold values from -0.15625 to 0.15625
- fc2_bias: bfloat16 [768], replicated, may hold values from -2 to 2
- cotangent: bfloat16 [32, 380, 768], P('clip', 'seq'), may hold values from -6 to 6
Outputs:
- block_out: bfloat16 [32, 380, 768], P('clip', 'seq')
- input_grad: bfloat16 [32, 380, 768], P('clip', 'seq')
- freq_table_grad: float32 [12, 768], replicated
- time_table_grad: float32 [99, 768], replicated
- norm1_gain_grad: float32 [768], replicated
- norm1_shift_grad: float32 [768], replicated
- qkv_weight_grad: float32 [768, 2304], P('clip')
- qv_bias_grad: float32 [2, 768], replicated
- proj_weight_grad: float32 [768, 768], P('clip')
- proj_bias_grad: float32 [768], replicated
- norm2_gain_grad: float32 [768], replicated
- norm2_shift_grad: float32 [768], replicated
- fc1_weight_grad: float32 [768, 3072], P('clip')
- fc1_bias_grad: float32 [3072], replicated
- fc2_weight_grad: float32 [3072, 768], P('clip')
- fc2_bias_grad: float32 [768], replicated
Inputs may be any that keep to these rules, and one draw needn't show every extreme that they name: `freq_index`: each clip's 7 frequency rows are distinct and increasing. `time_index`: each clip's 54 time columns are distinct and increasing.
All inputs are finite; a program needn't handle non-finite values.
Results may differ from a plain program's by a relative error of at most 0.012.
Values may be sent and summed in bfloat16 or wider, within the bound.
A program may use at most 192 MiB of HBM per device.

v0:
```python
import functools

import jax
import jax.numpy as jnp
from jax import lax
from jax.experimental import pallas as pl
from jax.experimental.pallas import tpu as pltpu
from jax.sharding import PartitionSpec as P

F32, BF16 = jnp.float32, jnp.bfloat16
MESH = pl.DeviceIdType.MESH
HDIM = 64
FKEEP = 7
TKEEP = 54
SPLIT = 4
GROUP = 8
PAD = 16
TIMES = 112
SLOTS = 64
BLOCK = 96
UNITS = 12
PARTS = tuple((i, 0, 3) for i in range(UNITS))
ORDER = (
    "out0", "out1", "t0_0", "gh0", "gh1", "t0_1", "gh2", "gh3", "sec", "out2", "t0_2", "sen", "att", "t1_1", "t1_0",
    "t0_3", "t0_4", "t0_5", "ab0", "t2_1", "t3_1", "t2_0", "ab1", "t3_0", "ab2", "t4_1", "t1_2", "t0_6", "fir",
    "t4_0", "fin", "t1_3", "t0_7", "t1_5", "t1_4", "t0_8", "t1_6", "t2_3", "t3_3", "t2_2", "t2_5", "t1_7", "t0_9",
    "t2_4", "t3_2", "t5_1", "t3_5", "t4_2", "t1_8", "t2_6", "t0_10", "t4_3", "tab", "t4_5", "t0_11", "t3_4", "t2_7",
    "t5_2", "t2_8", "t1_9", "t5_3", "t3_6", "t3_7", "t5_5", "t1_10", "t5_0", "t4_4", "t4_6", "t3_8", "pay2", "t4_7",
    "t1_11", "t2_9", "t4_8", "t2_11", "t2_10", "t5_4", "t3_9", "pay3", "t5_7", "t3_11", "t5_6", "t4_9", "t3_10",
    "t5_8", "t4_11", "t5_9", "t4_10", "t5_11", "t5_10",
)
NT = (((1,), (1,)), ((), ()))
TN = (((0,), (0,)), ((), ()))
LOG2_E = 1.4426950408889634
ERF_P = 0.3275911
ERF_C = (0.254829592, -0.284496736, 1.421413741, -1.453152027, 1.061405429)


def dot(a, b, dims=(((1,), (0,)), ((), ()))):
    return lax.dot_general(a, b, dims, preferred_element_type=F32)


def normal_cdf_pdf(h):
    bell = jnp.exp2(h * h * (-0.5 * LOG2_E))
    base = 1.0 + (ERF_P * 2.0**-0.5) * jnp.abs(h)
    t = pl.reciprocal(base, approx=True)
    t = t * (2.0 - base * t)
    tail = 0.5 * ERF_C[4]
    for coefficient in ERF_C[3::-1]:
        tail = tail * t + 0.5 * coefficient
    tail = tail * t * bell
    return jnp.where(h >= 0, 1.0 - tail, tail), bell * 0.3989422804014327


def normalize(v):
    centered = v - jnp.mean(v, -1, keepdims=True)
    rstd = lax.rsqrt(jnp.mean(centered * centered, -1, keepdims=True) + 1e-06)
    return centered * rstd, rstd


def row(ref):
    return ref[...].astype(F32).reshape(1, -1)


def block_kernel(
    tokens, freq_index_hbm, time_index_hbm, freq_table_hbm, time_table_hbm,
    gain1_hbm, shift1_hbm, qkv_hbm, qv_bias_hbm, proj_hbm, proj_bias_hbm, gain2_hbm, shift2_hbm,
    fc1_hbm, fc1_bias_hbm, fc2_hbm, fc2_bias_hbm, cotangent,
    out_hbm, grad_hbm, shares_hbm, small_hbm,
    freq_index, time_index, freq_table, time_table, gain1, shift1, qv_bias, proj_bias, gain2, shift2, fc1_bias, fc2_bias,
    raw, wide, w_qkv, w_proj, w_fc1, w_fc2, tok_in, cot_in, wide_cot, stream_in, normed, qkv, probs, attended, mid,
    work, left, right, unit, got1, got2, end_in, mid_in, final, staged, staged_grad,
    picks, pay, pay_low, pay_in, pay_mid, pay_out,
    v_sem, raw_sem, w_sem, tok_s, tok_r, cot_s, cot_r, out_s, out_r, grad_s, grad_r, left_s, left_r, right_s, right_r,
    one_s, one_r, two_s, two_r, end_s, end_r, mid_s, mid_r, fin_s, fin_r, share_s,
    pay_s, pay_r, payz_s, payz_r, payo_s, payo_r,
):
    width = stream_in.shape[1]
    rows = tok_in.shape[1]
    padded = stream_in.shape[0] // SPLIT
    many = stream_in.shape[0]
    shard = width // GROUP
    half = width // 2
    pairs = width // (2 * HDIM)
    heavy = 3 * width
    step = 256 if width % 256 == 0 else 128

    c, z = lax.axis_index("clip"), lax.axis_index("seq")
    low = c % GROUP
    core, x, y = low % 2, (low // 2) % 2, low // 4
    base = c - low

    def peer(bits):
        px = 1 - x if bits & 2 else x
        py = 1 - y if bits & 4 else y
        pc = 1 - core if bits & 1 else core
        return pc + 2 * px + 4 * py

    def at(bits):
        return (base + peer(bits), z)

    def near(d):
        places = (z, jnp.where(z % 2 == 0, z + 1, z - 1), jnp.where(z < 2, 2, 1), jnp.where(z < 2, 3, 0))
        if isinstance(d, int):
            return places[d]
        return jnp.where(d == 0, places[0], jnp.where(d == 1, places[1], jnp.where(d == 2, places[2], places[3])))

    def along(d):
        return (c, near(d))

    is_end = (z == 0) | (z == SPLIT - 1)
    is_mid = (z == 1) | (z == 2)
    to_mid = (c, jnp.where(z == 0, 1, 2))
    to_end = (c, jnp.where(z == 1, 0, 3))
    to_other = (c, jnp.where(z == 1, 2, 1))

    def remote(src, dst, send, recv, device):
        return pltpu.make_async_remote_copy(
            src_ref=src, dst_ref=dst, send_sem=send, recv_sem=recv, device_id=device, device_id_type=MESH
        )

    small = [
        pltpu.make_async_copy(src, dst, v_sem.at[i])
        for i, (src, dst) in enumerate(
            (
                (freq_index_hbm, freq_index), (time_index_hbm, time_index),
                (freq_table_hbm, freq_table), (time_table_hbm, time_table),
                (gain1_hbm, gain1), (shift1_hbm, shift1), (qv_bias_hbm, qv_bias), (proj_bias_hbm, proj_bias),
                (gain2_hbm, gain2), (shift2_hbm, shift2), (fc1_bias_hbm, fc1_bias), (fc2_bias_hbm, fc2_bias),
            )
        )
    ]
    weights = [
        pltpu.make_async_copy(src, dst, w_sem.at[i])
        for i, (src, dst) in enumerate(
            ((qkv_hbm, w_qkv), (proj_hbm, w_proj), (fc1_hbm, w_fc1), (fc2_hbm, w_fc2))
        )
    ]
    raw_tok = pltpu.make_async_copy(tokens, raw, raw_sem.at[0])
    raw_cot = pltpu.make_async_copy(cotangent, raw, raw_sem.at[1])
    raw_tok.start()
    for copy in weights[:2]:
        copy.start()
    barrier = pltpu.get_barrier_semaphore()
    for d in range(1, SPLIT):
        pl.semaphore_signal(barrier, inc=1, device_id=along(d), device_id_type=MESH)
    for bits in range(1, GROUP):
        pl.semaphore_signal(barrier, inc=1, device_id=at(bits), device_id_type=MESH)
    for copy in small:
        copy.start()

    chunks = range(0, width, step)

    def spread(src, dst, send, recv, n):
        here, i = pl.ds(n, step), n // step
        return [
            remote(src.at[near(d), :, here], dst.at[z, :, here], send.at[d - 1, i], recv.at[z, i], along(d))
            for d in range(SPLIT - 1, 0, -1)
        ]

    def keep(src, dst, recv, n):
        here = pl.ds(n, step)
        return pltpu.make_async_copy(src.at[z, :, here], dst.at[z, :, here], recv.at[z, n // step])

    def come(src, dst, send, recv, n, k):
        here, i = pl.ds(n, step), n // step
        return remote(src.at[k, :, here], dst.at[k, :, here], send.at[0, i], recv.at[k, i], along(1))

    def wait_block(src, dst, send, recv, n, k):
        @pl.when(z == k)
        def _():
            keep(src, dst, recv, n).wait()

        @pl.when(z != k)
        def _():
            come(src, dst, send, recv, n, k).wait_recv()

    def by_clip(staging, n):
        wide[...] = raw[:, :, pl.ds(n, step)].astype(F32)
        for k in range(SPLIT):
            staging[k, :, pl.ds(n, step)] = wide[:, k, :].astype(BF16)

    raw_tok.wait()
    for n in chunks:
        by_clip(staged, n)
        if n == 0:
            pl.semaphore_wait(barrier, SPLIT - 1 + GROUP - 1)
        for copy in spread(staged, tok_in, tok_s, tok_r, n):
            copy.start()
        keep(staged, tok_in, tok_r, n).start()
    raw_cot.start()
    raw_cot.wait()
    for copy in weights[2:]:
        copy.start()
    for n in chunks:
        by_clip(staged_grad, n)
        keep(staged_grad, cot_in, cot_r, n).start()
    for copy in small:
        copy.wait()

    lane = lax.broadcasted_iota(jnp.int32, (8, 128), 1)
    index = jnp.full((8, 128), -1, jnp.int32)
    for s in range(TKEEP):
        index = jnp.where(lane == s, time_index[z, s], index)
    for s in range(FKEEP):
        index = jnp.where(lane == SLOTS + s, freq_index[z, s] + TIMES, index)
    column = lax.broadcasted_iota(jnp.int32, (128, 128), 0)
    pick = jnp.where(column == index[:1], 1.0, 0.0)
    picks[...] = pick.astype(BF16)
    pay[...] = jnp.zeros_like(pay)
    pay[pl.ds(0, time_table.shape[0]), :] = time_table[...].astype(F32)
    pay[pl.ds(TIMES, freq_table.shape[0]), :] = freq_table[...].astype(F32)
    by_slot = dot(pick.T.astype(BF16), pay[...].astype(BF16)).astype(BF16)

    def slots_of(row_number, slot):
        block = sum((row_number >= padded * k).astype(jnp.int32) for k in range(1, SPLIT))
        inside = row_number - padded * block
        patch = row_number - (padded - rows) * block - 2
        frequency = sum((patch >= TKEEP * k).astype(jnp.int32) for k in range(1, FKEEP))
        time = patch - TKEEP * frequency
        hit = (slot == time) | (slot == SLOTS + frequency)
        return jnp.where(hit & (inside < rows) & (patch >= 0), 1.0, 0.0).astype(BF16)

    g1, s1 = row(gain1), row(shift1)
    bias_q, bias_v = qv_bias[0:1, :].astype(F32), qv_bias[1:2, :].astype(F32)
    weights[0].wait()
    @pl.loop(0, SPLIT)
    def _(d):
        k = near(d)
        place = pl.multiple_of(padded * k, 32)
        block_rows = pl.ds(place, padded)
        number = lax.broadcasted_iota(jnp.int32, (padded, 128), 0) + place
        slot = lax.broadcasted_iota(jnp.int32, (padded, 128), 1)
        position = dot(slots_of(number, slot), by_slot)
        for n in chunks:
            wait_block(staged, tok_in, tok_s, tok_r, n, k)
        stream_in[pl.ds(place, rows), :] = tok_in[k].astype(F32) + position[:rows]
        stream_in[pl.ds(place + rows, padded - rows), :] = jnp.zeros((padded - rows, width), F32)
        hat, _ = normalize(stream_in[block_rows, :])
        normed[block_rows, :] = (hat * g1 + s1).astype(BF16)
        for t, (bias, scale) in enumerate(((bias_q, HDIM**-0.5), (None, 1.0), (bias_v, 1.0))):
            for n in range(0, width, step):
                part = dot(normed[block_rows, :], w_qkv[:, pl.ds(t * width + n, step)])
                if bias is not None:
                    part = part + bias[:, n : n + step]
                part = part.astype(BF16)
                if scale != 1.0:
                    part = part * jnp.asarray(scale, BF16)
                qkv[block_rows, pl.ds(t * width + n, step)] = part

    for n in chunks:
        for copy in spread(staged_grad, cot_in, cot_s, cot_r, n):
            copy.start()
    part_of = [jnp.where(core == side, 0, 2) for side in range(2)]

    def left_copy(i):
        if i >= 4:
            return remote(left.at[2, i], left.at[1, i], left_s.at[i], left_r.at[i], at(1))
        return left_quarter(i)

    def left_quarter(q):
        return remote(
            left.at[2, pl.ds(0, 4), q], left.at[1, pl.ds(0, 4), q], left_s.at[q], left_r.at[q], at(1)
        )

    def blocks_in(n):
        found = []
        for block in range(n // shard, -(-(n + step) // shard)):
            found.append((block, max(n, shard * block), min(n + step, shard * (block + 1))))
        return found

    def hand_all(i, source):
        for n in range(0, width, step):
            turned = source[:, pl.ds(n, step)].T
            for block, start, stop in blocks_in(n):
                at_row = pl.ds(start - shard * block, stop - start)
                left[part_of[block % 2], i, block // 2, at_row, :] = turned[start - n : stop - n]
        left_copy(i).start()

    def right_copy(g):
        return remote(
            right.at[g, pl.ds(0, many)], right.at[g, pl.ds(many, many)], right_s.at[g], right_r.at[g], at(1)
        )

    hand_all(6, normed)

    key_number = lax.broadcasted_iota(jnp.int32, (8, many), 1)
    key_block = sum((key_number >= padded * k).astype(jnp.int32) for k in range(1, SPLIT))
    key_mask = jnp.where(key_number - padded * key_block < rows, 0.0, -1e30)[:1]
    head_lane = lax.broadcasted_iota(jnp.int32, (8, 2 * HDIM), 1)
    one_head = [
        jnp.where(head_lane < HDIM, 1.0, 0.0)[:1].astype(BF16),
        jnp.where(head_lane < HDIM, 0.0, 1.0)[:1].astype(BF16),
    ]

    def lanes(t, p):
        return pl.ds(pl.multiple_of(t * width + p * (2 * HDIM), 2 * HDIM), 2 * HDIM)

    def scores_of(p, place):
        query, key = qkv[:, lanes(0, p)], qkv[:, lanes(1, p)]
        for h in range(2):
            place[:, pl.ds(h * many, many)] = dot(query * one_head[h], key, NT)

    def weigh(p, place):
        value = qkv[:, lanes(2, p)]
        for r in range(0, many, 64):
            here = pl.ds(r, 64)
            for h in range(2):
                scores = place[here, pl.ds(h * many, many)] + key_mask
                weight = jnp.exp(scores - jnp.max(scores, -1, keepdims=True))
                weight = weight * (1.0 / jnp.sum(weight, -1, keepdims=True))
                probs[p, here, pl.ds(h * many, many)] = weight.astype(BF16)
        both = jnp.concatenate([value * one_head[0], value * one_head[1]], 0)
        attended[:, lanes(0, p)] = dot(probs[p], both).astype(BF16)

    scores_of(0, work)

    @pl.loop(0, pairs // 2)
    def _(m):
        scores_of(2 * m + 1, mid)
        weigh(2 * m, work)
        scores_of(jnp.minimum(2 * m + 2, pairs - 1), work)
        weigh(2 * m + 1, mid)

    weights[1].wait()
    hand_all(5, attended)
    bias = row(proj_bias)
    for n in range(0, width, step):
        mid[:, pl.ds(n, step)] = (
            stream_in[:, pl.ds(n, step)]
            + dot(attended[...], w_proj[:, pl.ds(n, step)])
            + bias[:, n : n + step]
        )
    g2, s2 = row(gain2), row(shift2)

    @pl.loop(0, many // BLOCK)
    def _(b):
        at_row = pl.ds(pl.multiple_of(b * BLOCK, BLOCK), BLOCK)
        hat, _ = normalize(mid[at_row, :])
        normed[at_row, :] = (hat * g2 + s2).astype(BF16)

    def column_sums(value):
        return jnp.sum(value.astype(F32), 0, keepdims=True)

    def first_matrix(q, n):
        place = pl.ds(pl.multiple_of(q * width + n, 128), step)
        work[:, pl.ds(n, step)] = dot(normed[...], w_fc1[:, place]) + fc1_bias[place].astype(F32).reshape(1, step)

    def activate(q, n):
        parts = []
        for r in range(0, many, 64):
            here = pl.ds(r, 64)
            hidden = work[here, pl.ds(n, step)]
            cdf, pdf = normal_cdf_pdf(hidden)
            active = (hidden * cdf).astype(BF16)
            unit[8 + q, here, pl.ds(n, step)] = active
            right[1 + q, here, pl.ds(n, step)] = (cdf + hidden * pdf).astype(BF16)
            parts.append(active)
        turned = jnp.concatenate(parts, 0).T
        for block, start, stop in blocks_in(n):
            at_row = pl.ds(start - shard * block, stop - start)
            left[part_of[block // 4], block % 4, q, at_row, :] = turned[start - n : stop - n]

    weights[2].wait()
    hand_all(4, normed)
    first_matrix(0, 0)

    def quarter(q, more):
        for n in range(step, width, step):
            first_matrix(q, n)
            activate(q, n - step)
        if more:
            first_matrix(q + 1, 0)
        activate(q, width - step)
        left_quarter(q).start()

    @pl.loop(0, 3)
    def _(q):
        quarter(q, True)

    wide_cot[pl.ds(rows, padded - rows), :] = jnp.zeros((padded - rows, step), F32)
    for k in range(SPLIT):
        for n in chunks:
            wait_block(staged_grad, cot_in, cot_s, cot_r, n, k)
            wide_cot[pl.ds(0, rows), :] = cot_in[k, :, pl.ds(n, step)].astype(F32)
            right[0, pl.ds(padded * k, padded), pl.ds(n, step)] = wide_cot[...].astype(BF16)
    for n in range(0, width, step):
        pay[pl.ds(99 + 7, 1), pl.ds(n, step)] = column_sums(right[0, pl.ds(0, many), pl.ds(n, step)])
    right_copy(0).start()

    quarter(3, False)

    def grid_of(j):
        return unit.at[PARTS[j][0]].reshape(2, 2, shard, width)

    def span(j, part):
        i, start, size = PARTS[j]
        size = size * width // 6
        return pl.ds(start * width // 6 + part * size, size)

    def some(j, part):
        i, start, size = PARTS[j]
        return pl.ds(start * width // 12, size * width // 6)

    def one_copies(j):
        u, i, here = grid_of(j), PARTS[j][0], some(j, 0)
        return (
            remote(u.at[:, 1 - x, :, span(j, 0)], got1.at[i, 0, :, :, here], one_s.at[j, 0], one_r.at[j, 0], at(2)),
            remote(u.at[1 - y, :, :, span(j, 1)], got1.at[i, 1, :, :, here], one_s.at[j, 1], one_r.at[j, 1], at(4)),
        )

    def two_copies(j):
        u, i, here = grid_of(j), PARTS[j][0], some(j, 0)
        return (
            remote(u.at[1 - y, x, :, span(j, 0)], got2.at[i, 0, :, here], two_s.at[j, 0], two_r.at[j, 0], at(4)),
            remote(u.at[y, 1 - x, :, span(j, 1)], got2.at[i, 1, :, here], two_s.at[j, 1], two_r.at[j, 1], at(2)),
        )

    own_part = jnp.where(z == 2, 1, 0)
    oth_part = 1 - own_part
    end_first = jnp.where(z < 2, 1, 0)

    def place_of(j, part):
        i, start, size = PARTS[j]
        size = size * width // 6
        return pl.ds(pl.multiple_of(start * width // 6 + part * size, 128), size)

    def end_copy(j, which):
        cols = place_of(j, end_first if which == 0 else 1 - end_first)
        i = PARTS[j][0]
        return remote(
            grid_of(j).at[y, x, :, cols], end_in.at[i, :, cols], end_s.at[j, which], end_r.at[j, which], to_mid
        )

    def mid_copy(j):
        return remote(
            grid_of(j).at[y, x, :, place_of(j, oth_part)], mid_in.at[PARTS[j][0], :, some(j, 0)], mid_s.at[j],
            mid_r.at[j], to_other,
        )

    def fin_copy(j, part, which, device):
        here = final.at[PARTS[j][0], :, place_of(j, part)]
        return remote(here, here, fin_s.at[j, which], fin_r.at[j, part], device)

    def share_copy(j):
        i, start, size = PARTS[j]
        cols = pl.ds(start * width // 6, size * width // 3)
        return pltpu.make_async_copy(final.at[i, :, cols], shares_hbm.at[i, :, cols], share_s.at[j])

    waited = set()

    def product(j):
        i, start, size = PARTS[j]
        l = i if i < 4 else 4 if i < 8 else 5 if i == 8 else 6
        g = 0 if i < 4 else i - 3
        for other in range(4) if l < 4 else (l,):
            if ("left", other) not in waited:
                left_copy(other).wait_recv()
                waited.add(("left", other))
        if g not in waited:
            right_copy(g).wait_recv()
            waited.add(g)
        both = jnp.concatenate([left[k, l].reshape(4 * shard, many) for k in range(2)], 1)
        for n in range(start * width // 6, (start + 2 * size) * width // 6, step):
            part = dot(both, right[g, :, pl.ds(n, step)])
            unit[i, :, pl.ds(n, step)] = part.astype(BF16)
        for copy in one_copies(j):
            copy.start()

    def tick1(j):
        u, i, here = grid_of(j), PARTS[j][0], some(j, 0)
        first, second = one_copies(j)
        after_first, after_second = two_copies(j)
        a, b = span(j, 0), span(j, 1)
        first.wait_recv()
        u[1 - y, x, :, a] = (u[1 - y, x, :, a].astype(F32) + got1[i, 0, 1 - y, :, here].astype(F32)).astype(BF16)
        after_first.start()
        second.wait_recv()
        u[y, 1 - x, :, b] = (u[y, 1 - x, :, b].astype(F32) + got1[i, 1, 1 - x, :, here].astype(F32)).astype(BF16)
        after_second.start()

    def plane_sum(j, part):
        i, here = PARTS[j][0], some(j, 0)
        near = jnp.where(part == 0, y, x)
        return (
            grid_of(j)[y, x, :, place_of(j, part)].astype(F32)
            + got1[i, part, near, :, here].astype(F32)
            + got2[i, part, :, here].astype(F32)
        )

    def tick2(j):
        for copy in two_copies(j):
            copy.wait_recv()

        @pl.when(is_end)
        def _():
            for which in range(2):
                part = end_first if which == 0 else 1 - end_first
                grid_of(j)[y, x, :, place_of(j, part)] = plane_sum(j, part).astype(BF16)
                end_copy(j, which).start()

    def line_sum(j, part):
        return plane_sum(j, part) + end_in[PARTS[j][0], :, place_of(j, part)].astype(F32)

    def tick3(j):
        @pl.when(is_mid)
        def _():
            end_copy(j, 0).wait_recv()
            grid_of(j)[y, x, :, place_of(j, oth_part)] = line_sum(j, oth_part).astype(BF16)
            mid_copy(j).start()

    def tick4(j):
        @pl.when(is_mid)
        def _():
            i = PARTS[j][0]
            end_copy(j, 1).wait_recv()
            total = line_sum(j, own_part)
            mid_copy(j).wait_recv()
            total = total + mid_in[i, :, some(j, 0)].astype(F32)
            final[i, :, place_of(j, own_part)] = total.astype(BF16)
            fin_copy(j, own_part, 0, to_other).start()
            fin_copy(j, own_part, 1, to_end).start()

    def tick5(j):
        @pl.when(is_mid)
        def _():
            fin_copy(j, oth_part, 2, to_end).wait_recv()
            fin_copy(j, oth_part, 2, to_end).start()

        @pl.when(is_end)
        def _():
            fin_copy(j, 0, 0, to_mid).wait_recv()
            fin_copy(j, 1, 0, to_mid).wait_recv()

        share_copy(j).start()

    bias_out = row(fc2_bias)

    def block_out(n):
        if n == 0:
            for m in chunks:
                for copy in spread(staged, tok_in, tok_s, tok_r, m):
                    copy.wait_send()
        part = mid[:, pl.ds(n, step)] + bias_out[:, n : n + step]
        for q in range(4):
            part = part + dot(unit[8 + q], w_fc2[pl.ds(q * width, width), pl.ds(n, step)])
        for k in range(SPLIT):
            staged[k, :, pl.ds(n, step)] = part[padded * k : padded * k + rows].astype(BF16)
        for copy in spread(staged, out_hbm, out_s, out_r, n):
            copy.start()
        keep(staged, out_hbm, out_r, n).start()

    def grad_hidden(q):
        for n in range(0, width, step):
            part = dot(right[0, pl.ds(0, many), :], w_fc2[pl.ds(q * width + n, step), :], NT)
            part = (part * right[1 + q, pl.ds(0, many), pl.ds(n, step)].astype(F32)).astype(BF16)
            right[1 + q, pl.ds(0, many), pl.ds(n, step)] = part
            pay[pl.ds(99 + 8 + q, 1), pl.ds(n, step)] = column_sums(part)
        right_copy(1 + q).start()

    def grad_second():
        for n in range(0, width, step):
            part = None
            for q in range(4):
                term = dot(right[1 + q, pl.ds(0, many), :], w_fc1[pl.ds(n, step), pl.ds(q * width, width)], NT)
                part = term if part is None else part + term
            work[:, pl.ds(n, step)] = part

    def norm_back(grad, value, gain):
        hat, rstd = normalize(value)
        g = grad * gain
        back = rstd * (g - jnp.mean(g, -1, keepdims=True) - hat * jnp.mean(g * hat, -1, keepdims=True))
        return back, hat

    zero = jnp.zeros((1, width), F32)

    def second_norm():
        def block(b, sums):
            at_row = pl.ds(pl.multiple_of(b * BLOCK, BLOCK), BLOCK)
            grad = work[at_row, :]
            back, hat = norm_back(grad, mid[at_row, :], g2)
            back = back + right[0, at_row, :].astype(F32)
            mid[at_row, :] = back
            branch = back.astype(BF16)
            right[5, at_row, :] = branch
            return (
                sums[0] + column_sums(grad * hat),
                sums[1] + column_sums(grad),
                sums[2] + column_sums(branch),
            )

        sums = lax.fori_loop(0, many // BLOCK, block, (zero, zero, zero))
        pay[pl.ds(99 + 5, 1), :] = sums[0]
        pay[pl.ds(99 + 6, 1), :] = sums[1]
        pay[pl.ds(99 + 4, 1), :] = sums[2]
        right_copy(5).start()

    def grad_attended():
        for n in range(0, width, step):
            normed[:, pl.ds(n, step)] = dot(
                right[5, pl.ds(0, many), :], w_proj[pl.ds(n, step), :], NT
            ).astype(BF16)

    def attend_back(p):
        query, key, value = (qkv[:, lanes(t, p)] for t in range(3))
        grad_out = normed[:, lanes(0, p)]
        grads = None
        for h in range(2):
            weight_low = probs[p, :, pl.ds(h * many, many)]
            weight = weight_low.astype(F32)
            grad_probs = dot(grad_out * one_head[h], value, NT) * weight
            inner = jnp.sum(grad_probs, -1, keepdims=True)
            grad_scores = (grad_probs - weight * inner).astype(BF16)
            terms = (
                dot(grad_scores, key * one_head[h]),
                dot(grad_scores, query * one_head[h], TN),
                dot(weight_low, grad_out * one_head[h], TN),
            )
            grads = terms if grads is None else tuple(a + b for a, b in zip(grads, terms, strict=True))
        for t, (grad, scale) in enumerate(zip(grads, (HDIM**-0.5, 1.0, 1.0), strict=True)):
            low_grad = (grad * scale).astype(BF16)
            right[6 + t, pl.ds(0, many), lanes(0, p)] = low_grad
            if t != 1:
                pay[pl.ds(99 + 2 + t // 2, 1), lanes(0, p)] = column_sums(low_grad)

    def attention_back(s):
        @pl.loop(s * pairs // 3, (s + 1) * pairs // 3)
        def _(p):
            attend_back(p)

        if s == 2:
            for t in range(3):
                right_copy(6 + t).start()

    def grad_first():
        for n in range(0, width, step):
            part = None
            for t in range(3):
                term = dot(right[6 + t, pl.ds(0, many), :], w_qkv[pl.ds(n, step), pl.ds(t * width, width)], NT)
                part = term if part is None else part + term
            work[:, pl.ds(n, step)] = part

    def own_grad():
        return pltpu.make_async_copy(staged_grad.at[z], grad_hbm.at[z], grad_r.at[z])

    def grad_copy(d):
        return remote(staged_grad.at[near(d)], grad_hbm.at[z], grad_s.at[d - 1], grad_r.at[z], along(d))

    def first_norm():
        for n in chunks:
            for copy in spread(staged_grad, cot_in, cot_s, cot_r, n):
                copy.wait_send()
        def block(t, sums):
            d = SPLIT - 1 - t
            k = near(d)
            at_row = pl.ds(pl.multiple_of(padded * k, 32), padded)
            grad = work[at_row, :]
            back, hat = norm_back(grad, stream_in[at_row, :], g1)
            back = mid[at_row, :] + back
            mid[at_row, :] = back
            staged_grad[k] = back[:rows].astype(BF16)

            @pl.when(d == 0)
            def _():
                own_grad().start()

            @pl.when(d > 0)
            def _():
                grad_copy(d).start()

            return sums[0] + column_sums(grad * hat), sums[1] + column_sums(grad)

        sums = lax.fori_loop(0, SPLIT, block, (zero, zero))
        first, second = sums
        pay[pl.ds(99, 1), :] = first
        pay[pl.ds(100, 1), :] = second

    def halves(v):
        high = v.astype(BF16)
        return high, (v - high.astype(F32)).astype(BF16)

    def pay_copy(bits):
        return remote(
            pay_low.at[pl.ds(16 * peer(bits), 16)], pay_in.at[low], pay_s.at[bits - 1], pay_r.at[low], at(bits)
        )

    def payz_copy(d):
        return remote(pay_mid.at[z], pay_mid.at[z], payz_s.at[d - 1], payz_r.at[z], along(d))

    def payo_copy(bits):
        return remote(pay_out.at[low], pay_out.at[low], payo_s.at[bits - 1], payo_r.at[low], at(bits))

    def position_tables():
        number = lax.broadcasted_iota(jnp.int32, (128, many), 1)
        slot = lax.broadcasted_iota(jnp.int32, (128, many), 0)
        slots = slots_of(number, slot)
        for n in range(0, width, step):
            by = sum(dot(slots, v) for v in halves(mid[:, pl.ds(n, step)]))
            table_grad = sum(dot(picks[...], v) for v in halves(by))
            pay[pl.ds(0, 99), pl.ds(n, step)] = table_grad[:99]
            pay[pl.ds(TIMES, 16), pl.ds(n, step)] = table_grad[TIMES:]
        pay[pl.ds(111, 1), :] = zero
        pay_low[...] = pay[...].astype(BF16)
        for bits in range(1, GROUP):
            pay_copy(bits).start()

    def pay_group():
        for bits in range(1, GROUP):
            remote(
                pay_low.at[pl.ds(0, 16)], pay_in.at[peer(bits)], pay_s.at[bits - 1], pay_r.at[peer(bits)], at(bits)
            ).wait_recv()
        pay_in[low] = pay_low[pl.ds(pl.multiple_of(16 * low, 16), 16), :]
        pay_mid[z] = sum(pay_in[s].astype(F32) for s in range(GROUP)).astype(BF16)
        for d in range(1, SPLIT):
            payz_copy(d).start()

    def pay_line():
        for d in range(1, SPLIT):
            k = near(d)
            remote(pay_mid.at[k], pay_mid.at[k], payz_s.at[d - 1], payz_r.at[k], along(d)).wait_recv()
        pay_out[low] = sum(pay_mid[s].astype(F32) for s in range(SPLIT)).astype(BF16)
        for bits in range(1, GROUP):
            payo_copy(bits).start()

    pieces = {
        "sec": grad_second, "sen": second_norm, "att": grad_attended, "fir": grad_first,
        "fin": first_norm, "tab": position_tables, "pay2": pay_group, "pay3": pay_line,
    }
    for n in chunks:
        pieces[f"out{n // step}"] = functools.partial(block_out, n)
    for q in range(4):
        pieces[f"gh{q}"] = functools.partial(grad_hidden, q)
    for s in range(3):
        pieces[f"ab{s}"] = functools.partial(attention_back, s)
    for i in range(len(PARTS)):
        pieces[f"t0_{i}"] = functools.partial(product, i)
        for k, tick in enumerate((tick1, tick2, tick3, tick4, tick5)):
            pieces[f"t{k + 1}_{i}"] = functools.partial(tick, i)
    assert sorted(ORDER) == sorted(pieces)
    weights[3].wait()
    for name in ORDER:
        pieces[name]()
    for bits in range(1, GROUP):
        remote(
            pay_out.at[low], pay_out.at[peer(bits)], payo_s.at[bits - 1], payo_r.at[peer(bits)], at(bits)
        ).wait_recv()
    last = pltpu.make_async_copy(pay_out, small_hbm, w_sem.at[0])
    last.start()

    for n in chunks:
        for copy in spread(staged, out_hbm, out_s, out_r, n):
            copy.wait_send()
        for k in range(SPLIT):
            wait_block(staged, out_hbm, out_s, out_r, n, k)
    own_grad().wait()
    for d in range(1, SPLIT):
        grad_copy(d).wait_send()
        k = near(d)
        remote(staged_grad.at[k], grad_hbm.at[k], grad_s.at[0], grad_r.at[k], along(1)).wait_recv()
    for i in range(left.shape[1]):
        left_copy(i).wait_send()
    for g in range(right.shape[0]):
        right_copy(g).wait_send()

    for j in range(len(PARTS)):
        for copy in (*one_copies(j), *two_copies(j)):
            copy.wait_send()

    @pl.when(is_end)
    def _():
        for j in range(len(PARTS)):
            end_copy(j, 0).wait_send()
            end_copy(j, 1).wait_send()

    @pl.when(is_mid)
    def _():
        for j in range(len(PARTS)):
            mid_copy(j).wait_send()
            fin_copy(j, own_part, 0, to_other).wait_send()
            fin_copy(j, own_part, 1, to_end).wait_send()
            fin_copy(j, oth_part, 2, to_end).wait_send()

    for j in range(len(PARTS)):
        share_copy(j).wait()

    for bits in range(1, GROUP):
        pay_copy(bits).wait_send()
        payo_copy(bits).wait_send()
    for d in range(1, SPLIT):
        payz_copy(d).wait_send()
    last.wait()


def finish_kernel(
    out_in, grad_in, shares, small,
    out, grad, freq, time, gain1, shift1, qkv, qv_bias, proj, proj_bias, gain2, shift2, fc1, fc1_bias, fc2, fc2_bias,
    rows_in, wide, rows_out, parts, small_in, f_qkv, f_proj, f_fc1, f_fc2, f_time, f_freq, f_qv, lines,
    row_sem, part_sem, out_sem,
):
    width = wide.shape[2]
    shard = parts.shape[1]
    reads = [pltpu.make_async_copy(shares.at[i], parts.at[i], part_sem.at[i]) for i in range(UNITS)]
    moves = [pltpu.make_async_copy(src, rows_in.at[i], row_sem.at[i]) for i, src in enumerate((out_in, grad_in))]
    read_small = pltpu.make_async_copy(small, small_in, row_sem.at[2])
    for copy in (*reads, *moves, read_small):
        copy.start()
    line_of = lambda i: lines.at[pl.ds(i * width, width)]
    writes = [
        pltpu.make_async_copy(src, dst, out_sem.at[i])
        for i, (src, dst) in enumerate(
            (
                (f_fc2, fc2), (f_fc1, fc1), (f_proj, proj), (f_qkv, qkv), (rows_out.at[0], out), (rows_out.at[1], grad),
                (f_time, time), (f_freq, freq), (f_qv, qv_bias), (line_of(0), gain1), (line_of(1), shift1),
                (line_of(2), proj_bias), (line_of(3), gain2), (line_of(4), shift2), (line_of(5), fc2_bias),
                (lines.at[pl.ds(6 * width, 4 * width)], fc1_bias),
            )
        )
    ]
    for i in range(UNITS):
        reads[i].wait()
        value = parts[i].astype(F32)
        if i < 4:
            f_fc2[pl.ds(i * shard, shard), :] = value
        elif i < 8:
            f_fc1[:, pl.ds((i - 4) * width, width)] = value
        elif i == 8:
            f_proj[...] = value
        else:
            f_qkv[:, pl.ds((i - 9) * width, width)] = value
        if i in (3, 7, 8, 11):
            writes[(3, 7, 8, 11).index(i)].start()
    for i in range(2):
        moves[i].wait()
        for k in range(SPLIT):
            wide[:, k, :] = rows_in[i, k].astype(F32)
        rows_out[i] = wide[...].astype(BF16)
        writes[4 + i].start()
    read_small.wait()
    f_time[...] = small_in[pl.ds(0, time.shape[0]), :].astype(F32)
    f_freq[...] = small_in[pl.ds(TIMES, freq.shape[0]), :].astype(F32)
    rest = small_in[pl.ds(96, 16), :].astype(F32)[3:]
    f_qv[...] = rest[2:4]
    for at, i in enumerate((0, 1, 4, 5, 6, 7)):
        lines[pl.ds(at * width, width)] = rest[i : i + 1].reshape(width)
    for q in range(4):
        lines[pl.ds((6 + q) * width, width)] = rest[8 + q : 9 + q].reshape(width)
    for copy in writes[6:]:
        copy.start()
    for copy in writes:
        copy.wait()


def on_device(
    tokens, freq_index, time_index, freq_table, time_table,
    norm1_gain, norm1_shift, qkv_weight, qv_bias, proj_weight, proj_bias, norm2_gain, norm2_shift,
    fc1_weight, fc1_bias, fc2_weight, fc2_bias, cotangent,
):
    clips, rows, width = tokens.shape
    count = len(PARTS)
    pieces = width // (256 if width % 256 == 0 else 128)
    times, freqs = time_table.shape[0], freq_table.shape[0]
    groups = lax.axis_size("seq")
    clip_devices = lax.axis_size("clip")
    assert clips == SPLIT and groups == SPLIT and clip_devices % GROUP == 0
    hidden_width = fc1_weight.shape[1]
    assert hidden_width == 4 * width
    padded = -(-rows // 32) * 32
    many = SPLIT * padded
    shard = width // GROUP
    half = width // 2
    heads = width // HDIM

    anywhere = pl.BlockSpec(memory_space=pl.ANY)
    dma = pltpu.SemaphoreType.DMA
    blocks = (SPLIT, rows, width)
    vectors = (freq_table, time_table, norm1_gain, norm1_shift, qv_bias, proj_bias, norm2_gain, norm2_shift, fc1_bias, fc2_bias)
    small_scratch = [pltpu.SMEM(v.shape, v.dtype) for v in (freq_index, time_index)]
    small_scratch += [pltpu.VMEM(v.shape, v.dtype) for v in vectors]
    tokens, cotangent = (v.transpose(1, 0, 2) for v in (tokens, cotangent))
    out, grad, shares, small = pl.pallas_call(
        block_kernel,
        out_shape=(
            jax.ShapeDtypeStruct(blocks, BF16),
            jax.ShapeDtypeStruct(blocks, BF16),
            jax.ShapeDtypeStruct((UNITS, shard, width), BF16),
            jax.ShapeDtypeStruct((GROUP, 16, width), BF16),
        ),
        in_specs=[anywhere] * 18,
        out_specs=(anywhere,) * 4,
        scratch_shapes=[
            *small_scratch,
            pltpu.VMEM((rows, SPLIT, width), BF16),
            pltpu.VMEM((rows, SPLIT, 256 if width % 256 == 0 else 128), F32),
            pltpu.VMEM((width, 3 * width), BF16),
            pltpu.VMEM((width, width), BF16),
            pltpu.VMEM((width, hidden_width), BF16),
            pltpu.VMEM((hidden_width, width), BF16),
            pltpu.VMEM(blocks, BF16),
            pltpu.VMEM(blocks, BF16),
            pltpu.VMEM((padded, 256 if width % 256 == 0 else 128), F32),
            pltpu.VMEM((many, width), F32),
            pltpu.VMEM((many, width), BF16),
            pltpu.VMEM((many, 3 * width), BF16),
            pltpu.VMEM((heads // 2, many, 2 * many), BF16),
            pltpu.VMEM((many, width), BF16),
            pltpu.VMEM((many, width), F32),
            pltpu.VMEM((many, width), F32),
            pltpu.VMEM((3, 7, 4, shard, many), BF16),
            pltpu.VMEM((9, 2 * many, width), BF16),
            pltpu.VMEM((UNITS, 4 * shard, width), BF16),
            pltpu.VMEM((UNITS, 2, 2, shard, half), BF16),
            pltpu.VMEM((UNITS, 2, shard, half), BF16),
            pltpu.VMEM((UNITS, shard, width), BF16),
            pltpu.VMEM((UNITS, shard, half), BF16),
            pltpu.VMEM((UNITS, shard, width), BF16),
            pltpu.VMEM(blocks, BF16),
            pltpu.VMEM(blocks, BF16),
            pltpu.VMEM((128, 128), BF16),
            pltpu.VMEM((128, width), F32),
            pltpu.VMEM((128, width), BF16),
            pltpu.VMEM((GROUP, 16, width), BF16),
            pltpu.VMEM((SPLIT, 16, width), BF16),
            pltpu.VMEM((GROUP, 16, width), BF16),
            dma((12,)), dma((2,)), dma((4,)),
            dma((3, pieces)), dma((4, pieces)), dma((3, pieces)), dma((4, pieces)), dma((3, pieces)), dma((4, pieces)),
            dma((3,)), dma((4,)),
            dma((7,)), dma((7,)), dma((9,)), dma((9,)),
            dma((count, 2)), dma((count, 2)), dma((count, 2)), dma((count, 2)),
            dma((count, 2)), dma((count, 2)), dma((count,)), dma((count,)),
            dma((count, 3)), dma((count, 2)), dma((count,)),
            dma((7,)), dma((8,)), dma((3,)), dma((4,)), dma((7,)), dma((8,)),
        ],
        compiler_params=pltpu.CompilerParams(
            collective_id=1, has_side_effects=True, vmem_limit_bytes=63 * 2**20
        ),
    )(
        tokens, freq_index, time_index, freq_table, time_table,
        norm1_gain, norm1_shift, qkv_weight, qv_bias, proj_weight, proj_bias, norm2_gain, norm2_shift,
        fc1_weight, fc1_bias, fc2_weight, fc2_bias, cotangent,
    )
    small = small.reshape(GROUP * 16, width)
    if clip_devices == GROUP:
        shape = lambda *dims: jax.ShapeDtypeStruct(dims, F32)
        inner = jax.ShapeDtypeStruct((rows, SPLIT, width), BF16)
        line = shape(width)
        results = (
            inner, inner, shape(freqs, width), shape(times, width), line, line, shape(shard, 3 * width),
            shape(2, width), shape(shard, width), line, line, line, shape(shard, 4 * width),
            shape(4 * width), shape(4 * shard, width), line,
        )
        out, grad, *others = pl.pallas_call(
            finish_kernel,
            out_shape=results,
            in_specs=[anywhere] * 4,
            out_specs=(anywhere,) * 16,
            scratch_shapes=[
                pltpu.VMEM((2, *blocks), BF16),
                pltpu.VMEM((rows, SPLIT, width), F32),
                pltpu.VMEM((2, rows, SPLIT, width), BF16),
                pltpu.VMEM((UNITS, shard, width), BF16),
                pltpu.VMEM((GROUP * 16, width), BF16),
                pltpu.VMEM((shard, 3 * width), F32),
                pltpu.VMEM((shard, width), F32),
                pltpu.VMEM((shard, 4 * width), F32),
                pltpu.VMEM((4 * shard, width), F32),
                pltpu.VMEM((times, width), F32),
                pltpu.VMEM((freqs, width), F32),
                pltpu.VMEM((2, width), F32),
                pltpu.VMEM((10 * width,), F32),
                dma((3,)), dma((UNITS,)), dma((16,)),
            ],
            compiler_params=pltpu.CompilerParams(vmem_limit_bytes=62 * 2**20),
        )(out, grad, shares, small)
        return (out.transpose(1, 0, 2), grad.transpose(1, 0, 2), *others)
    shares, small = shares.astype(F32), small.astype(F32)
    wide_count = clip_devices // GROUP
    same = [[h * GROUP + b for h in range(wide_count)] for b in range(GROUP)]
    small = lax.psum(small, "clip", axis_index_groups=same)
    fc2 = shares[:4].reshape(4 * shard, width)
    rest = shares[4:].transpose(1, 0, 2).reshape(shard, 8 * width)
    summed = [
        lax.psum_scatter(v, "clip", scatter_dimension=0, axis_index_groups=same, tiled=True)
        for v in (fc2, rest)
    ]
    moves = [(h * GROUP + b, b * wide_count + h) for h in range(wide_count) for b in range(GROUP)]
    fc2, rest = (lax.ppermute(v, "clip", moves) for v in summed)
    fc1, proj, qkv = rest[:, : 4 * width], rest[:, 4 * width : 5 * width], rest[:, 5 * width :]
    return (
        out,
        grad,
        small[TIMES : TIMES + freqs],
        small[:times],
        small[99],
        small[100],
        qkv,
        small[101:103],
        proj,
        small[103],
        small[104],
        small[105],
        fc1,
        small[107:111].reshape(-1),
        fc2,
        small[106],
    )


def solution(mesh):
    rows_split, clip_split = P("clip", "seq", None), P("clip", None)
    in_specs = (rows_split, clip_split, clip_split) + (P(),) * 14 + (rows_split,)
    out_specs = (
        rows_split, rows_split, P(), P(), P(), P(), clip_split, P(), clip_split, P(), P(), P(), clip_split,
        P(), clip_split, P(),
    )
    return jax.shard_map(on_device, mesh=mesh, in_specs=in_specs, out_specs=out_specs, check_vma=False)
```

profile of v0, /device:TPU:0, one launch (start us, length us, event | category | flops | bytes accessed | tf_op | source)
XLA Modules:
  0.0 130.2 jit_solution(11327073446312153259)
XLA Ops:
  0.7 125.3 %shard_map.297 = (bf16[4,95,768]{2,1,0:T(8,128)(2,1)}, bf16[4,95,768]{2,1,0:T(8,128)(2,1)}, bf16[12,96,768]{2,1,0:T(8,128)(2,1)}, bf16[8,16,768]{2,1,0:T(8,128)(2,1)}) custom-call(bf16[95,4,768]{2,1,0:T(4,128)(2,1)} %bitcast.5, s32[4,7]{1,0:T(4,128)} %freq_index_hbm.1, s32[4,54]{1,0:T(4,128)} %time_index_hbm.1, bf16[12,768]{1,0:T(8,128)(2,1)} %freq_table_hbm.1, ...), custom_call_target="tpu_custom_call" | custom-call | tf_op jit(solution)/shard_map/pallas_call | solution.py:880
  125.9 4.0 %shard_map.298 = (bf16[95,4,768]{2,1,0:T(4,128)(2,1)}, bf16[95,4,768]{2,1,0:T(4,128)(2,1)}, f32[12,768]{1,0:T(8,128)}, f32[99,768]{1,0:T(8,128)}, f32[768]{0:T(1...) custom-call(bf16[4,95,768]{2,1,0:T(8,128)(2,1)} %get-tuple-element.3, ...), custom_call_target="tpu_custom_call" | custom-call | tf_op jit(solution)/shard_map/pallas_call | solution.py:951
where the time goes:
time: 130 us
  Pallas kernels  129 us (99%)
    pallas_call x1, Pallas kernels, on_device(): pl.pallas_call(block_kernel, out_shape=(jax.ShapeDtypeStruct(blocks, BF16...  125 us
    pallas_call x1, Pallas kernels, on_device(): pl.pallas_call(finish_kernel, out_shape=results, in_specs=[anywhere] * 4,...  4.02 us

commit v1 on v0

--- a/solution.py
+++ b/solution.py
@@ -738,7 +738,35 @@
             pieces[f"t{k + 1}_{i}"] = functools.partial(tick, i)
     assert sorted(ORDER) == sorted(pieces)
     weights[3].wait()
-    for name in ORDER:
+    def finished():
+        for n in chunks:
+            for copy in spread(staged, out_hbm, out_s, out_r, n):
+                copy.wait_send()
+            for k in range(SPLIT):
+                wait_block(staged, out_hbm, out_s, out_r, n, k)
+        own_grad().wait()
+        for d in range(1, SPLIT):
+            grad_copy(d).wait_send()
+            k = near(d)
+            remote(staged_grad.at[k], grad_hbm.at[k], grad_s.at[0], grad_r.at[k], along(1)).wait_recv()
+        for i in range(left.shape[1]):
+            left_copy(i).wait_send()
+        for g in range(right.shape[0]):
+            right_copy(g).wait_send()
+
+        for j in range(len(PARTS)):
+            for copy in (*one_copies(j), *two_copies(j)):
+                copy.wait_send()
+
+        @pl.when(is_end)
+        def _():
+            for j in range(len(PARTS)):
+                end_copy(j, 0).wait_send()
+                end_copy(j, 1).wait_send()
+
+    for number, name in enumerate(ORDER):
+        if number == len(ORDER) - 3:
+            finished()
         pieces[name]()
     for bits in range(1, GROUP):
         remote(
@@ -746,31 +774,6 @@
         ).wait_recv()
     last = pltpu.make_async_copy(pay_out, small_hbm, w_sem.at[0])
     last.start()
-
-    for n in chunks:
-        for copy in spread(staged, out_hbm, out_s, out_r, n):
-            copy.wait_send()
-        for k in range(SPLIT):
-            wait_block(staged, out_hbm, out_s, out_r, n, k)
-    own_grad().wait()
-    for d in range(1, SPLIT):
-        grad_copy(d).wait_send()
-        k = near(d)
-        remote(staged_grad.at[k], grad_hbm.at[k], grad_s.at[0], grad_r.at[k], along(1)).wait_recv()
-    for i in range(left.shape[1]):
-        left_copy(i).wait_send()
-    for g in range(right.shape[0]):
-        right_copy(g).wait_send()
-
-    for j in range(len(PARTS)):
-        for copy in (*one_copies(j), *two_copies(j)):
-            copy.wait_send()
-
-    @pl.when(is_end)
-    def _():
-        for j in range(len(PARTS)):
-            end_copy(j, 0).wait_send()
-            end_copy(j, 1).wait_send()
 
     @pl.when(is_mid)
     def _():

time: 130 us -> 130 us (level)
  no operation moved by 1% of the time
where the time goes in v1:
time: 130 us
  Pallas kernels  129 us (99%)
    pallas_call x1, Pallas kernels, on_device(): pl.pallas_call(block_kernel, out_shape=(jax.ShapeDtypeStruct(blocks, BF16...  125 us
    pallas_call x1, Pallas kernels, on_device(): pl.pallas_call(finish_kernel, out_shape=results, in_specs=[anywhere] * 4,...  4.02 us

profile of v1, /device:TPU:0, one launch (start us, length us, event | category | flops | bytes accessed | tf_op | source)
XLA Modules:
  0.0 130.1 jit_solution(5156135480236196220)
XLA Ops:
  0.7 125.3 %shard_map.297 = (bf16[4,95,768]{2,1,0:T(8,128)(2,1)}, bf16[4,95,768]{2,1,0:T(8,128)(2,1)}, bf16[12,96,768]{2,1,0:T(8,128)(2,1)}, bf16[8,16,768]{2,1,0:T(8,128)(2,1)}) custom-call(bf16[95,4,768]{2,1,0:T(4,128)(2,1)} %bitcast.5, s32[4,7]{1,0:T(4,128)} %freq_index_hbm.1, s32[4,54]{1,0:T(4,128)} %time_index_hbm.1, bf16[12,768]{1,0:T(8,128)(2,1)} %freq_table_hbm.1, ...), custom_call_target="tpu_custom_call" | custom-call | tf_op jit(solution)/shard_map/pallas_call | solution.py:883
  125.9 4.0 %shard_map.298 = (bf16[95,4,768]{2,1,0:T(4,128)(2,1)}, bf16[95,4,768]{2,1,0:T(4,128)(2,1)}, f32[12,768]{1,0:T(8,128)}, f32[99,768]{1,0:T(8,128)}, f32[768]{0:T(1...) custom-call(bf16[4,95,768]{2,1,0:T(8,128)(2,1)} %get-tuple-element.3, ...), custom_call_target="tpu_custom_call" | custom-call | tf_op jit(solution)/shard_map/pallas_call | solution.py:954
